TPU v7x, 32 devices: a whole 2x2x4 slice. The times are simulated.
32 devices in a mesh: dp: 4 (over x, core), seq: 8 (over z, y).
Axes of the slice: x: 2, y: 2, z: 4, core: 2. Of those that a mesh axis runs over, the one named last changes fastest.
Arguments:
- voxels: bfloat16 [4, 1024, 4096], P('dp', 'seq'), may hold values from -6 to 6
- patch_weight: bfloat16 [4096, 1024], replicated, may hold values from -0.09375 to 0.09375
- patch_bias: float32 [1024], replicated, may hold values from -3 to 3
- enc_position: bfloat16 [1024, 1024], P('seq'), may hold values from -5 to 5
- visible: int32 [4, 1024], P('dp', 'seq'), may hold values from 0 to 1, as said below
- enc_project: bfloat16 [1024, 3072], P(('dp', 'seq')), may hold values from -1 to 1
- enc_merge: bfloat16 [1024, 1024], P(('dp', 'seq')), may hold values from -0.1875 to 0.1875
- dec_lift: bfloat16 [1024, 512], P(('dp', 'seq')), may hold values from -0.1875 to 0.1875
- mask_token: float32 [512], replicated, may hold values from -4 to 4
- dec_position: bfloat16 [1024, 512], P('seq'), may hold values from -5 to 5
- dec_project: bfloat16 [512, 1536], P(('dp', 'seq')), may hold values from -1 to 1
- dec_merge: bfloat16 [512, 512], P(('dp', 'seq')), may hold values from -0.25 to 0.25
- dec_predict: bfloat16 [512, 4096], P(('dp', 'seq')), may hold values from -0.25 to 0.25
Outputs:
- decoded: bfloat16 [4, 1024, 512], P('dp', 'seq')
- patch_loss: float32 [4, 1024], P('dp', 'seq')
Inputs may be any that keep to these rules, and one draw needn't show every extreme that they name: `visible`: each cube has exactly 256 ones. Each slab of 128 consecutive patches holds between 0 and 64 ones, and in every cube some slab holds exactly 64.
All inputs are finite; a program needn't handle non-finite values.
Results may differ from a plain program's by a relative error of at most 0.008.
Values may be sent and summed in bfloat16 or wider, within the bound.
A program may use at most 128 MiB of HBM per device.

v0:
```python
import math

import jax
import jax.numpy as jnp
from jax import lax
from jax.sharding import PartitionSpec as P

ENC_HEADS = 16
DEC_HEADS = 16


def layer_norm(values):
    centre = values - jnp.mean(values, axis=-1, keepdims=True)
    spread = jnp.mean(centre * centre, axis=-1, keepdims=True)
    return centre * lax.rsqrt(spread + 1e-06)


def attend_rows(queries, key_rows, value_rows, key_ok):
    query_rows, local_heads, head_size = queries.shape
    block_rows = math.gcd(query_rows, 512)
    score_scale = 1.0 / math.sqrt(head_size)
    head_outputs = []
    for head_index in range(local_heads):
        query_blocks = queries[:, head_index].reshape(
            query_rows // block_rows, block_rows, head_size
        )
        keys_one = key_rows[:, head_index]
        values_one = value_rows[:, head_index]

        def one_block(query_block):
            scores = (
                jnp.einsum("qd,kd->qk", query_block, keys_one, preferred_element_type=jnp.float32)
                * score_scale
            )
            if key_ok is not None:
                scores = jnp.where(key_ok[None, :], scores, -1e30)
            top_score = jnp.max(scores, axis=-1, keepdims=True)
            exponent = jnp.exp(scores - top_score)
            weights = (exponent / jnp.sum(exponent, axis=-1, keepdims=True)).astype(jnp.bfloat16)
            return jnp.einsum(
                "qk,kd->qd", weights, values_one, preferred_element_type=jnp.float32
            ).astype(jnp.bfloat16)

        head_outputs.append(lax.map(one_block, query_blocks).reshape(query_rows, head_size))
    return jnp.stack(head_outputs, axis=1)


def spread_heads(packed, heads, seq_count):
    row_count = packed.shape[0]
    head_size = packed.shape[1] // (3 * heads)
    query_parts = max(seq_count // heads, 1)
    local_heads = max(heads // seq_count, 1)
    layout = packed.reshape(row_count, 3, heads, head_size)
    if query_parts > 1:
        layout = jnp.repeat(layout, query_parts, axis=2)
    layout = layout.reshape(row_count, 3, seq_count, local_heads, head_size).transpose(
        2, 0, 1, 3, 4
    )
    return layout.reshape(seq_count, row_count, 3 * local_heads * head_size)


def attend_heads(incoming, key_ok, heads, query_part, query_parts):
    sources, row_count, triple_width = incoming.shape
    local_heads = max(heads // sources, 1)
    head_size = triple_width // (3 * local_heads)
    all_rows = sources * row_count
    layout = incoming.reshape(all_rows, 3, local_heads, head_size)
    query_rows = all_rows // query_parts
    queries = lax.dynamic_slice_in_dim(layout[:, 0], query_part * query_rows, query_rows, 0)
    return attend_rows(queries, layout[:, 1], layout[:, 2], key_ok)


def place_rows(mixed_part, all_rows, query_part, sources):
    query_rows = mixed_part.shape[0]
    flat_part = mixed_part.reshape(query_rows, -1)
    buffer = jnp.zeros((all_rows, flat_part.shape[1]), jnp.bfloat16)
    buffer = lax.dynamic_update_slice(buffer, flat_part, (query_part * query_rows, 0))
    return buffer.reshape(sources, all_rows // sources, flat_part.shape[1])


def collect_heads(returned, heads, query_parts):
    sources, row_count, piece_width = returned.shape
    local_heads = max(heads // sources, 1)
    head_size = piece_width // local_heads
    arranged = returned.reshape(sources, row_count, local_heads, head_size).transpose(1, 0, 2, 3)
    arranged = arranged.reshape(row_count, heads, query_parts, head_size)
    summed = jnp.sum(arranged.astype(jnp.float32), axis=2).astype(jnp.bfloat16)
    return summed.reshape(row_count, heads * head_size)


def shards(
    voxels,
    patch_weight,
    patch_bias,
    enc_position,
    visible,
    enc_project,
    enc_merge,
    dec_lift,
    mask_token,
    dec_position,
    dec_project,
    dec_merge,
    dec_predict,
):
    seq_count = lax.axis_size("seq")
    seq_place = lax.axis_index("seq")
    enc_parts = max(seq_count // ENC_HEADS, 1)
    dec_parts = max(seq_count // DEC_HEADS, 1)
    enc_part = seq_place % enc_parts
    dec_part = seq_place % dec_parts
    full_project, full_merge, full_lift = (
        lax.all_gather(enc_project, ("dp", "seq"), axis=0, tiled=True),
        lax.all_gather(enc_merge, ("dp", "seq"), axis=0, tiled=True),
        lax.all_gather(dec_lift, ("dp", "seq"), axis=0, tiled=True),
    )
    tok_local = voxels.shape[1]
    slab_max = tok_local // 2
    slot_ids = jnp.arange(slab_max, dtype=jnp.int32)
    cube_index = 0
    cube_flags = visible[cube_index]
    embedded = (
        jnp.dot(voxels[cube_index], patch_weight, preferred_element_type=jnp.float32)
        + patch_bias
        + enc_position.astype(jnp.float32)
    ).astype(jnp.bfloat16)
    ranking = jnp.cumsum(cube_flags) - 1
    slot_index = jnp.where(cube_flags == 1, ranking, slab_max)
    chooser = (slot_index[None, :] == slot_ids[:, None]).astype(jnp.bfloat16)
    kept_rows = jnp.dot(chooser, embedded, preferred_element_type=jnp.float32).astype(jnp.bfloat16)
    present = slot_ids < jnp.sum(cube_flags)
    packed = jnp.dot(
        layer_norm(kept_rows.astype(jnp.float32)).astype(jnp.bfloat16),
        full_project,
        preferred_element_type=jnp.float32,
    ).astype(jnp.bfloat16)
    key_marks = jnp.broadcast_to(present.astype(jnp.bfloat16)[None, :], (seq_count, slab_max))
    outgoing = spread_heads(packed, ENC_HEADS, seq_count)
    incoming = lax.all_to_all(outgoing, "seq", split_axis=0, concat_axis=0, tiled=True)
    in_marks = lax.all_to_all(key_marks, "seq", split_axis=0, concat_axis=0, tiled=True)
    key_ok = in_marks.reshape(-1) > 0.5
    mixed_part = attend_heads(incoming, key_ok, ENC_HEADS, enc_part, enc_parts)
    returning = place_rows(mixed_part, incoming.shape[0] * incoming.shape[1], enc_part, seq_count)
    returned = lax.all_to_all(returning, "seq", split_axis=0, concat_axis=0, tiled=True)
    mixed_rows = collect_heads(returned, ENC_HEADS, enc_parts)
    encoded = kept_rows.astype(jnp.float32) + jnp.dot(
        mixed_rows, full_merge, preferred_element_type=jnp.float32
    )
    lifted_list = [
        jnp.dot(
            layer_norm(encoded).astype(jnp.bfloat16), full_lift, preferred_element_type=jnp.float32
        )
    ]
    rank_list = [ranking]
    dec_weights = (
        lax.all_gather(dec_project, ("dp", "seq"), axis=0, tiled=True),
        lax.all_gather(dec_merge, ("dp", "seq"), axis=0, tiled=True),
        lax.all_gather(dec_predict, ("dp", "seq"), axis=0, tiled=True),
    )
    cube_index = 0
    cube_flags = visible[cube_index]
    taken_rows = jnp.take(
        lifted_list[cube_index], jnp.clip(rank_list[cube_index], 0, slab_max - 1), axis=0
    )
    dec_in = (
        jnp.where(cube_flags[:, None] == 1, taken_rows, mask_token[None, :])
        + dec_position.astype(jnp.float32)
    ).astype(jnp.bfloat16)
    dec_packed = jnp.dot(
        layer_norm(dec_in.astype(jnp.float32)).astype(jnp.bfloat16),
        dec_weights[0],
        preferred_element_type=jnp.float32,
    ).astype(jnp.bfloat16)
    outgoing = spread_heads(dec_packed, DEC_HEADS, seq_count)
    incoming = lax.all_to_all(outgoing, "seq", split_axis=0, concat_axis=0, tiled=True)
    mixed_part = attend_heads(incoming, None, DEC_HEADS, dec_part, dec_parts)
    returning = place_rows(mixed_part, incoming.shape[0] * incoming.shape[1], dec_part, seq_count)
    returned = lax.all_to_all(returning, "seq", split_axis=0, concat_axis=0, tiled=True)
    mixed_rows = collect_heads(returned, DEC_HEADS, dec_parts)
    decoded = (
        dec_in.astype(jnp.float32)
        + jnp.dot(mixed_rows, dec_weights[1], preferred_element_type=jnp.float32)
    ).astype(jnp.bfloat16)
    predicted = jnp.dot(
        layer_norm(decoded.astype(jnp.float32)).astype(jnp.bfloat16),
        dec_weights[2],
        preferred_element_type=jnp.float32,
    )
    target = layer_norm(voxels[cube_index].astype(jnp.float32))
    squared = jnp.mean((predicted - target) * (predicted - target), axis=-1)
    loss_list = [jnp.where(cube_flags == 1, jnp.zeros_like(squared), squared)]
    decoded_list = [decoded]
    return (jnp.stack(decoded_list), jnp.stack(loss_list))


def solution(mesh):
    return jax.shard_map(
        shards,
        mesh=mesh,
        in_specs=(
            P("dp", "seq", None),
            P(),
            P(),
            P("seq", None),
            P("dp", "seq"),
            P(("dp", "seq"), None),
            P(("dp", "seq"), None),
            P(("dp", "seq"), None),
            P(),
            P("seq", None),
            P(("dp", "seq"), None),
            P(("dp", "seq"), None),
            P(("dp", "seq"), None),
        ),
        out_specs=(P("dp", "seq", None), P("dp", "seq")),
        check_vma=False,
    )
```

profile of v0, /device:TPU:0, one launch (start us, length us, event | category | flops | bytes accessed | tf_op | source)
XLA Modules:
  0.0 368.5 jit_solution(5729269688306685991)
XLA Ops:
  7.2 0.7 all-gather.6.cloned.1.call-update
  7.9 0.7 all-gather.8.cloned.1.call-update
  8.7 0.7 all-gather.10.cloned.1.call-update
  9.4 0.5 all-gather.12.cloned.1.call-update
  10.0 0.8 copy.32
  11.0 1.3 fusion.62
  12.3 0.6 compare_convert_fusion
  13.0 0.6 broadcast_in_dim.107
  13.6 7.3 %all-to-all-start = ((bf16[8,1,64]{2,1,0:T(2,128)(2,1)}), bf16[8,1,64]{2,1,0:T(2,128)(2,1)S(1)}, u32[]{:S(2)}, u32[]{:S(2)}) async-start(bf16[8,1,64]{2,1,0:T(2,128)(2,1)} %broadcast_in_dim.107), calls=%async_computation | async-start | bytes 8192 | tf_op jit(solution)/shard_map/all_to_all | solution.py:140
  20.9 5.3 %fusion.63 = (f32[64]{0:T(128)S(1)}, f32[64,1024]{1,0:T(8,128)S(1)}) fusion(bf16[4096,1024]{1,0:T(8,128)(2,1)} %param.18, bf16[1,128,4096]{2,1,0:T(8,128)(2,1)} %param.17, bf16[128,1024]{1,0:T(8,128)(2,1)} %param.20, f32[1024]{0:T(1024)} %param.19, s32[128]{0:T(128)S(1)} %get-tuple-element.156), kind=kOutput, calls=%fused_computation.133 | convolution fusion | flops 1091248128 | bytes 9966336 | tf_op jit(solution)/shard_map/dot_general | solution.py:130
  26.4 56.8 %all-gather.6.cloned.1.call-done = bf16[1024,3072]{1,0:T(8,128)(2,1)} async-done(((bf16[32,3072]{1,0:T(8,128)(2,1)}), bf16[1024,3072]{1,0:T(8,128)(2,1)}) %all-gather.6.cloned.1.call-update) | async-done | bytes 6291472 | tf_op jit(solution)/shard_map/all_gather | solution.py:113
  83.2 4.0 %convolution_convert_fusion.2 = bf16[64,3072]{1,0:T(8,128)(2,1)S(1)} fusion(bf16[1024,3072]{1,0:T(8,128)(2,1)} %all-gather.6.cloned.1.call-done, f32[64,1024]{1,0:T(8,128)S(1)} %get-tuple-element.158, f32[64]{0:T(128)S(1)} %add_rsqrt_fusion.4, f32[64]{0:T(128)S(1)} %broadcast_multiply_fusion.4), kind=kOutput, calls=%fused_computation.27 | convolution fusion | flops 403046400 | bytes 6947328 | tf_op jit(solution)/shard_map/dot_general | solution.py:132
  87.7 0.5 copy.58
  88.3 1.2 reshape.207
  89.5 4.0 %all-to-all-start.1 = ((bf16[8,64,384]{2,1,0:T(8,128)(2,1)}), bf16[8,64,384]{2,1,0:T(8,128)(2,1)S(1)}, u32[]{:S(2)}, u32[]{:S(2)}) async-start(bf16[8,64,384]{2,1,0:T(8,128)(2,1)} %reshape.207), calls=%async_computation.1 | async-start | bytes 786432 | tf_op jit(solution)/shard_map/all_to_all | solution.py:139
  93.6 0.5 all-gather.14.cloned.1.call-update
  94.2 12.7 %all-to-all-done.1 = bf16[8,64,384]{2,1,0:T(8,128)(2,1)S(1)} async-done(((bf16[8,64,384]{2,1,0:T(8,128)(2,1)}), bf16[8,64,384]{2,1,0:T(8,128)(2,1)S(1)}, u32[]{:S(2)}, u32[]{:S(2)}) %all-to-all-start.1) | async-done | bytes 393248 | tf_op jit(solution)/shard_map/all_to_all | solution.py:139
  107.3 0.5 fusion.60
  110.3 0.8 copy.35
  111.2 3.6 all-to-all-start.2
  114.8 8.1 %all-to-all-done.2 = bf16[8,64,128]{2,1,0:T(8,128)(2,1)S(1)} async-done(((bf16[8,64,128]{2,1,0:T(8,128)(2,1)}), bf16[8,64,128]{2,1,0:T(8,128)(2,1)S(1)}, u32[]{:S(2)}, u32[]{:S(2)}) %all-to-all-start.2) | async-done | bytes 131104 | tf_op jit(solution)/shard_map/all_to_all | solution.py:144
  123.4 20.2 %all-gather.8.cloned.1.call-done = bf16[1024,1024]{1,0:T(8,128)(2,1)} async-done(((bf16[32,1024]{1,0:T(8,128)(2,1)}), bf16[1024,1024]{1,0:T(8,128)(2,1)}) %all-gather.8.cloned.1.call-update) | async-done | bytes 2097168 | tf_op jit(solution)/shard_map/all_gather | solution.py:114
  143.6 2.2 fusion.68
  146.0 53.4 %all-gather.10.cloned.1.call-done = bf16[1024,512]{1,0:T(8,128)(2,1)} async-done(((bf16[32,512]{1,0:T(8,128)(2,1)}), bf16[1024,512]{1,0:T(8,128)(2,1)}) %all-gather.10.cloned.1.call-update) | async-done | bytes 1048592 | tf_op jit(solution)/shard_map/all_gather | solution.py:115
  199.4 1.6 fusion.45
  200.9 0.8 gather_fusion
  202.1 54.0 %all-gather.12.cloned.1.call-done = bf16[512,1536]{1,0:T(8,128)(2,1)} async-done(((bf16[16,1536]{1,0:T(8,128)(2,1)}), bf16[512,1536]{1,0:T(8,128)(2,1)}) %all-gather.12.cloned.1.call-update) | async-done | bytes 1572880 | tf_op jit(solution)/shard_map/all_gather | solution.py:156
  256.1 1.8 convolution_convert_fusion.3
  258.2 0.8 copy.38
  259.0 4.4 %all-to-all-start.3 = ((bf16[8,128,192]{1,2,0:T(8,128)(2,1)}), bf16[8,128,192]{1,2,0:T(8,128)(2,1)S(1)}, u32[]{:S(2)}, u32[]{:S(2)}) async-start(bf16[8,128,192]{1,2,0:T(8,128)(2,1)} %bitcast.23), calls=%async_computation.3 | async-start | bytes 786432 | tf_op jit(solution)/shard_map/all_to_all | solution.py:175
  263.6 73.7 %all_gather.22 = bf16[512,512]{1,0:T(8,128)(2,1)S(1)} all-gather(bf16[16,512]{1,0:T(8,128)(2,1)S(1)} %copy-done.3), channel_id=1, replica_groups=mesh['dp'=4,'seq'=8] {'dp','seq'}, dimensions={0}, use_global_device_ids=true | all-gather | bytes 540672 | tf_op jit(solution)/shard_map/all_gather | solution.py:157
  338.4 3.5 while.4
  338.4 0.5 multiply_reduce_fusion.6
  338.9 0.5 fusion.92
  339.4 0.7 fusion.93
  340.1 0.5 multiply_reduce_fusion.6
  340.6 0.5 fusion.92
  341.2 0.7 fusion.93
  342.5 3.4 while.5
  343.0 0.5 fusion.96
  343.6 0.7 fusion.97
  344.2 0.5 multiply_reduce_fusion.7
  344.8 0.5 fusion.96
  345.3 0.7 fusion.97
  346.1 0.7 copy.48
  346.8 3.4 all-to-all-start.4
  350.6 6.8 %all-to-all-done.4 = bf16[8,128,64]{1,2,0:T(8,128)(2,1)S(1)} async-done(((bf16[8,128,64]{1,2,0:T(8,128)(2,1)}), bf16[8,128,64]{1,2,0:T(8,128)(2,1)S(1)}, u32[]{:S(2)}, u32[]{:S(2)}) %all-to-all-start.4) | async-done | bytes 131104 | tf_op jit(solution)/shard_map/all_to_all | solution.py:178
  358.0 3.4 fusion.20
  (83 shorter events, 9.5 us)
Async XLA Ops:
  7.2 76.0 %all-gather.6.cloned.1.call-start = ((), (), s32[]{:S(2)}) async-start(), calls=%async_computation.5 | async-start | bytes 6488064 | tf_op jit(solution)/shard_map/all_gather | solution.py:113
  7.9 135.7 %all-gather.8.cloned.1.call-start = ((), (), s32[]{:S(2)}) async-start(), calls=%async_computation.6 | async-start | bytes 2162688 | tf_op jit(solution)/shard_map/all_gather | solution.py:114
  8.6 190.7 %all-gather.10.cloned.1.call-start = ((), (), s32[]{:S(2)}) async-start(), calls=%async_computation.7 | async-start | bytes 1081344 | tf_op jit(solution)/shard_map/all_gather | solution.py:115
  9.4 246.7 %all-gather.12.cloned.1.call-start = ((), (), s32[]{:S(2)}) async-start(), calls=%async_computation.8 | async-start | bytes 1622016 | tf_op jit(solution)/shard_map/all_gather | solution.py:156
  13.6 75.9 %all-to-all-start = ((bf16[8,1,64]{2,1,0:T(2,128)(2,1)}), bf16[8,1,64]{2,1,0:T(2,128)(2,1)S(1)}, u32[]{:S(2)}, u32[]{:S(2)}) async-start(bf16[8,1,64]{2,1,0:T(2,128)(2,1)} %broadcast_in_dim.107), calls=%async_computation | async-start | bytes 8192 | tf_op jit(solution)/shard_map/all_to_all | solution.py:140
  87.7 6.4 %copy-start.5 = (s32[1,128]{1,0:T(1,128)S(1)}, s32[1,128]{1,0:T(1,128)}, u32[]{:S(2)}) copy-start(s32[1,128]{1,0:T(1,128)} %param.21) | copy-start | bytes 1540
  89.5 17.4 %all-to-all-start.1 = ((bf16[8,64,384]{2,1,0:T(8,128)(2,1)}), bf16[8,64,384]{2,1,0:T(8,128)(2,1)S(1)}, u32[]{:S(2)}, u32[]{:S(2)}) async-start(bf16[8,64,384]{2,1,0:T(8,128)(2,1)} %reshape.207), calls=%async_computation.1 | async-start | bytes 786432 | tf_op jit(solution)/shard_map/all_to_all | solution.py:139
  93.5 264.5 %all-gather.14.cloned.1.call-start = ((), (), s32[]{:S(2)}) async-start(), calls=%async_computation.9 | async-start | bytes 4325376 | tf_op jit(solution)/shard_map/all_gather | solution.py:158
  111.2 11.7 %all-to-all-start.2 = ((bf16[8,64,128]{2,1,0:T(8,128)(2,1)}), bf16[8,64,128]{2,1,0:T(8,128)(2,1)S(1)}, u32[]{:S(2)}, u32[]{:S(2)}) async-start(bf16[8,64,128]{2,1,0:T(8,128)(2,1)} %copy.35), calls=%async_computation.2 | async-start | bytes 262144 | tf_op jit(solution)/shard_map/all_to_all | solution.py:144
  145.8 55.9 %copy-start.2 = (bf16[128,512]{1,0:T(8,128)(2,1)S(1)}, bf16[128,512]{1,0:T(8,128)(2,1)}, u32[]{:S(2)}) copy-start(bf16[128,512]{1,0:T(8,128)(2,1)} %param.26) | copy-start | bytes 393220
  145.8 55.9 %copy-start.4 = (f32[512]{0:T(512)S(1)}, f32[512]{0:T(512)}, u32[]{:S(2)}) copy-start(f32[512]{0:T(512)} %param.25) | copy-start | bytes 6148
  202.1 61.2 %copy-start = (bf16[1,128,4096]{2,1,0:T(8,128)(2,1)S(1)}, bf16[1,128,4096]{2,1,0:T(8,128)(2,1)}, u32[]{:S(2)}) copy-start(bf16[1,128,4096]{2,1,0:T(8,128)(2,1)} %param.17) | copy-start | bytes 3145732
  257.9 5.7 %copy-start.3 = (bf16[16,512]{1,0:T(8,128)(2,1)S(1)}, bf16[16,512]{1,0:T(8,128)(2,1)}, u32[]{:S(2)}) copy-start(bf16[16,512]{1,0:T(8,128)(2,1)} %param.28) | copy-start | bytes 49156
  259.0 78.3 %all-to-all-start.3 = ((bf16[8,128,192]{1,2,0:T(8,128)(2,1)}), bf16[8,128,192]{1,2,0:T(8,128)(2,1)S(1)}, u32[]{:S(2)}, u32[]{:S(2)}) async-start(bf16[8,128,192]{1,2,0:T(8,128)(2,1)} %bitcast.23), calls=%async_computation.3 | async-start | bytes 786432 | tf_op jit(solution)/shard_map/all_to_all | solution.py:175
  346.8 10.7 %all-to-all-start.4 = ((bf16[8,128,64]{1,2,0:T(8,128)(2,1)}), bf16[8,128,64]{1,2,0:T(8,128)(2,1)S(1)}, u32[]{:S(2)}, u32[]{:S(2)}) async-start(bf16[8,128,64]{1,2,0:T(8,128)(2,1)} %copy.48), calls=%async_computation.4 | async-start | bytes 262144 | tf_op jit(solution)/shard_map/all_to_all | solution.py:178
  357.8 3.6 copy-start.1
Sparse Core Ops, SparseCore 0:
  10.9 72.2 all-gather.5
  86.1 57.4 all-gather.7
  146.7 52.6 all-gather.9
  202.1 53.9 all-gather.11
  259.0 63.5 all-gather.13
where the time goes:
time: 369 us; the launch traced here: 368 us
  waiting for transfers between devices  215 us (58%)
  blocking collectives  73.7 us (20%)
  matrix products  24.7 us (7%)
  starting transfers between devices  22.8 us (6%)
  between operations  14.2 us (4%)
  local copies, waits for them, and re-layouts  10.9 us (3%)
  other arithmetic  7.05 us (2%)
    all_gather x1, blocking collectives, shards(): lax.all_gather(dec_merge, ('dp', 'seq'), axis=0, tiled=True)  73.7 us
    all_gather x1, waiting for transfers between devices, shards(): lax.all_gather(enc_project, ('dp', 'seq'), axis=0, tiled=True)  56.8 us
    all_gather x1, waiting for transfers between devices, shards(): lax.all_gather(dec_project, ('dp', 'seq'), axis=0, tiled=True)  54 us
    all_gather x1, waiting for transfers between devices, shards(): lax.all_gather(dec_lift, ('dp', 'seq'), axis=0, tiled=True)  53.4 us
    all_gather x1, waiting for transfers between devices, shards(): lax.all_gather(enc_merge, ('dp', 'seq'), axis=0, tiled=True)  20.2 us
    all_to_all x2, waiting for transfers between devices, shards(): lax.all_to_all(returning, 'seq', split_axis=0, concat_axis=0, tiled=True)  14.9 us
    all_to_all x2, waiting for transfers between devices, shards(): lax.all_to_all(outgoing, 'seq', split_axis=0, concat_axis=0, tiled=True)  12.7 us
    all_to_all x2, starting transfers between devices, shards(): lax.all_to_all(outgoing, 'seq', split_axis=0, concat_axis=0, tiled=True)  8.39 us
  transfers between devices with their start and end apart: 10, of which 7 were waited for; matrix products, arithmetic and copies ran while one was open for 11% of the time, Pallas kernels for 0%

commit v1 on v0

--- a/solution.py
+++ b/solution.py
@@ -3,6 +3,8 @@
 import jax
 import jax.numpy as jnp
 from jax import lax
+from jax.experimental import pallas as pl
+from jax.experimental.pallas import tpu as pltpu
 from jax.sharding import PartitionSpec as P
 
 ENC_HEADS = 16
@@ -193,9 +195,472 @@
     return (jnp.stack(decoded_list), jnp.stack(loss_list))
 
 
+def norm_rows(values):
+    centre = values - jnp.mean(values, axis=-1, keepdims=True)
+    spread = jnp.mean(centre * centre, axis=-1, keepdims=True)
+    return centre * lax.rsqrt(spread + 1e-06)
+
+
+def dot32(left, right):
+    return jnp.dot(left, right, preferred_element_type=jnp.float32)
+
+
+def dot_nt(left, right):
+    return lax.dot_general(
+        left, right, (((1,), (1,)), ((), ())), preferred_element_type=jnp.float32
+    )
+
+
+PIECES = 4
+SENDS = 160
+MESH = pl.DeviceIdType.MESH
+
+
+def fused(
+    vox_hbm,
+    pw_hbm,
+    bias_ref,
+    epos_hbm,
+    vis_ref,
+    eproj_hbm,
+    emerge_hbm,
+    lift_hbm,
+    mask_ref,
+    dpos_hbm,
+    dproj_hbm,
+    dmerge_hbm,
+    pred_hbm,
+    dec_out,
+    loss_out,
+    vx,
+    pw,
+    ep,
+    dpo,
+    flags_buf,
+    we,
+    wd,
+    pos,
+    bm,
+    bl,
+    bd,
+    bp,
+    e_buf,
+    x_buf,
+    m1,
+    r1,
+    m2,
+    r2,
+    qm,
+    qkv,
+    lsem,
+    ssem,
+    rsem,
+):
+    dp = lax.axis_index("dp")
+    sq = lax.axis_index("seq")
+    x, c = dp // 2, dp % 2
+    z, y = sq // 2, sq % 2
+    seq_peers = [(sq + j) % 8 for j in range(1, 8)]
+    z_peers = [((z + k) % 4) * 2 + y for k in range(1, 4)]
+    z_from = [(z + 4 - k) % 4 for k in range(1, 4)]
+    y_dev = (dp, z * 2 + 1 - y)
+    x_dev = ((1 - x) * 2 + c, sq)
+    c_dev = (x * 2 + 1 - c, sq)
+
+    counter = [0]
+    sent = []
+
+    def send(src, dst, device):
+        index = counter[0]
+        counter[0] += 1
+        copy = pltpu.make_async_remote_copy(
+            src_ref=src,
+            dst_ref=dst,
+            send_sem=ssem.at[index],
+            recv_sem=rsem.at[index],
+            device_id=device,
+            device_id_type=MESH,
+        )
+        copy.start()
+        sent.append(copy)
+        return copy
+
+    local_count = [0]
+
+    def local(src, dst):
+        index = local_count[0]
+        local_count[0] += 1
+        copy = pltpu.make_async_copy(src, dst, lsem.at[index])
+        copy.start()
+        return copy
+
+    def landed(copies):
+        for copy in copies:
+            copy.wait_recv()
+
+    vox_copy = local(vox_hbm, vx)
+    rows_piece = 4096 // PIECES
+    pw_copies = [
+        local(pw_hbm.at[pl.ds(i * rows_piece, rows_piece)], pw.at[pl.ds(i * rows_piece, rows_piece)])
+        for i in range(PIECES)
+    ]
+    ep_copy = local(epos_hbm, ep)
+    dpo_copy = local(dpos_hbm, dpo)
+    own = []
+    for third in range(3):
+        own.append(
+            local(
+                eproj_hbm.at[:, pl.ds(pl.multiple_of(third * 1024 + sq * 128, 128), 128)],
+                we.at[third, x, c, sq],
+            )
+        )
+        own.append(
+            local(
+                dproj_hbm.at[:, pl.ds(pl.multiple_of(third * 512 + z * 128, 128), 128)],
+                wd.at[third, x, c, sq],
+            )
+        )
+    own.append(local(dpos_hbm.at[pl.ds(pl.multiple_of(dp * 32, 32), 32)], pos.at[x, c, sq]))
+    for part, buf in ((emerge_hbm, bm), (lift_hbm, bl), (dmerge_hbm, bd), (pred_hbm, bp)):
+        own.append(local(part, buf.at[x, c, z, y]))
+
+    flag_row = vis_ref[...].astype(jnp.float32)
+    flags_buf[sq] = jnp.broadcast_to(flag_row, (8, 128))
+
+    barrier = pltpu.get_barrier_semaphore()
+    for peer in seq_peers:
+        pl.semaphore_signal(barrier, inc=1, device_id=(dp, peer), device_id_type=MESH)
+    pl.semaphore_signal(barrier, inc=1, device_id=x_dev, device_id_type=MESH)
+    pl.semaphore_signal(barrier, inc=1, device_id=c_dev, device_id_type=MESH)
+    pl.semaphore_wait(barrier, 9)
+
+    we_in, wd_in, pos_in, flags_in = [], [], [], []
+    for peer in seq_peers:
+        for third in range(3):
+            we_in.append(
+                send(
+                    eproj_hbm.at[:, pl.ds(pl.multiple_of(third * 1024 + peer * 128, 128), 128)],
+                    we.at[third, x, c, sq],
+                    (dp, peer),
+                )
+            )
+    for peer in seq_peers:
+        flags_in.append(send(flags_buf.at[sq], flags_buf.at[sq], (dp, peer)))
+
+    def z_stage(part, buf):
+        return [send(part, buf.at[x, c, z, y], (dp, peer)) for peer in z_peers]
+
+    bm_in = z_stage(emerge_hbm, bm)
+    bl_in = z_stage(lift_hbm, bl)
+    for peer in seq_peers:
+        for third in range(3):
+            wd_in.append(
+                send(
+                    dproj_hbm.at[
+                        :, pl.ds(pl.multiple_of(third * 512 + (peer // 2) * 128, 128), 128)
+                    ],
+                    wd.at[third, x, c, sq],
+                    (dp, peer),
+                )
+            )
+    for peer in seq_peers:
+        pos_in.append(
+            send(
+                dpos_hbm.at[pl.ds(pl.multiple_of(dp * 32, 32), 32)], pos.at[x, c, sq], (dp, peer)
+            )
+        )
+
+    tok_col = lax.broadcasted_iota(jnp.int32, (128, 128), 0)
+    tok_row = lax.broadcasted_iota(jnp.int32, (128, 128), 1)
+    upto = (tok_col <= tok_row).astype(jnp.bfloat16)
+    slot_col = lax.broadcasted_iota(jnp.int32, (64, 128), 0).astype(jnp.float32)
+
+    def chooser_of(row):
+        rank = dot32(jnp.broadcast_to(row, (8, 128)).astype(jnp.bfloat16), upto)[0:1] - 1.0
+        return jnp.where(
+            (jnp.broadcast_to(rank, (64, 128)) == slot_col)
+            & (jnp.broadcast_to(row, (64, 128)) > 0.5),
+            1.0,
+            0.0,
+        )
+
+    chooser = chooser_of(flag_row).astype(jnp.bfloat16)
+    vox_copy.wait()
+    total = jnp.zeros((128, 1024), jnp.float32)
+    for i in range(PIECES):
+        pw_copies[i].wait()
+        total = total + dot32(
+            vx[:, i * rows_piece : (i + 1) * rows_piece],
+            pw[i * rows_piece : (i + 1) * rows_piece, :],
+        )
+    ep_copy.wait()
+    embedded = (total + bias_ref[...] + ep[...].astype(jnp.float32)).astype(jnp.bfloat16)
+    kept = dot32(chooser, embedded)
+    e_buf[z, y] = norm_rows(kept).astype(jnp.bfloat16)
+
+    e_z = [send(e_buf.at[z, y], e_buf.at[z, y], (dp, peer)) for peer in z_peers]
+    e_y = [send(e_buf.at[z, y], e_buf.at[z, y], y_dev)]
+
+    for copy in own:
+        copy.wait()
+    landed(we_in)
+    we_x = send(we.at[:, x, c], we.at[:, x, c], x_dev)
+
+    vox32 = vx[...].astype(jnp.float32)
+    vox_mean = jnp.mean(vox32, axis=-1, keepdims=True)
+    vox_centre = vox32 - vox_mean
+    vox_scale = lax.rsqrt(jnp.mean(vox_centre * vox_centre, axis=-1, keepdims=True) + 1e-06)
+
+    for k in range(3):
+        e_z[k].wait_recv()
+        e_y.append(send(e_buf.at[z_from[k], y], e_buf.at[z_from[k], y], y_dev))
+    we_x.wait_recv()
+    we_c = send(we.at[:, :, c], we.at[:, :, c], c_dev)
+    landed(bm_in)
+    bm_y = send(bm.at[x, c, :, y], bm.at[x, c, :, y], y_dev)
+    landed(bl_in)
+    bl_y = send(bl.at[x, c, :, y], bl.at[x, c, :, y], y_dev)
+    landed(wd_in)
+    wd_x = send(wd.at[:, x, c], wd.at[:, x, c], x_dev)
+    landed(pos_in)
+    pos_x = send(pos.at[x, c], pos.at[x, c], x_dev)
+    landed(flags_in)
+    flags_all = jnp.max(flags_buf[...], axis=1)
+    counts = jnp.sum(flags_all, axis=1, keepdims=True)
+    lane512 = lax.broadcasted_iota(jnp.int32, (8, 512), 1)
+    slab512 = lax.broadcasted_iota(jnp.int32, (8, 512), 0)
+    count_row = jnp.sum(
+        jnp.where(lane512 // 64 == slab512, jnp.broadcast_to(counts, (8, 512)), 0.0),
+        axis=0,
+        keepdims=True,
+    )
+    key_ok = (lane512[0:1] % 64).astype(jnp.float32) < count_row
+    landed(e_y)
+    bm_y.wait_recv()
+    bm_x = send(bm.at[x, c], bm.at[x, c], x_dev)
+    bl_y.wait_recv()
+    bl_x = send(bl.at[x, c], bl.at[x, c], x_dev)
+    bd_in = z_stage(dmerge_hbm, bd)
+    bp_in = z_stage(pred_hbm, bp)
+    wd_x.wait_recv()
+    wd_c = send(wd.at[:, :, c], wd.at[:, :, c], c_dev)
+    pos_x.wait_recv()
+    pos_c = send(pos.at[:, c], pos.at[:, c], c_dev)
+    we_c.wait_recv()
+
+    rows_in = e_buf[...].reshape(512, 1024)
+    q_all, k_all, v_all = (
+        dot32(rows_in, we[third].reshape(1024, 128)).astype(jnp.bfloat16) for third in range(3)
+    )
+    lane128 = lax.broadcasted_iota(jnp.int32, (512, 128), 1)
+    results = []
+    for head in range(2):
+        mine = lane128 // 64 == head
+        q_one = jnp.where(mine, q_all, jnp.zeros_like(q_all))
+        v_one = jnp.where(mine, v_all, jnp.ones_like(v_all))
+        scores = dot_nt(q_one, k_all) * (1.0 / 8.0)
+        scores = jnp.where(jnp.broadcast_to(key_ok, (512, 512)), scores, -1e30)
+        top = jnp.max(scores, axis=-1, keepdims=True)
+        weights = jnp.exp(scores - top).astype(jnp.bfloat16)
+        summed = dot32(weights, v_one)
+        spot = 64 * (1 - head)
+        results.append(summed / summed[:, spot : spot + 1])
+    m1[...] = (
+        jnp.where(lane128 < 64, results[0], results[1]).astype(jnp.bfloat16).reshape(8, 64, 128)
+    )
+    r1[sq] = m1[sq]
+    r1_in = [send(m1.at[peer], r1.at[sq], (dp, peer)) for peer in seq_peers]
+
+    bm_x.wait_recv()
+    bm_c = send(bm.at[:, c], bm.at[:, c], c_dev)
+    bl_x.wait_recv()
+    bl_c = send(bl.at[:, c], bl.at[:, c], c_dev)
+    wd_c.wait_recv()
+    pos_c.wait_recv()
+    wd_all = jnp.concatenate([wd[third].reshape(512, 128) for third in range(3)], axis=1)
+    mask_row = mask_ref[...]
+
+    def masked_slab(slab, carry):
+        slab_pos = pos[:, :, slab].reshape(128, 512).astype(jnp.float32)
+        slab_in = (mask_row + slab_pos).astype(jnp.bfloat16).astype(jnp.float32)
+        qm[slab] = dot32(norm_rows(slab_in).astype(jnp.bfloat16), wd_all).astype(jnp.bfloat16)
+        return carry
+
+    lax.fori_loop(0, 8, masked_slab, 0)
+    landed(bp_in)
+    bp_x = send(bp.at[x, c, :, y], bp.at[x, c, :, y], x_dev)
+    landed(bd_in)
+    bd_y = send(bd.at[x, c, :, y], bd.at[x, c, :, y], y_dev)
+    dpo_copy.wait()
+    own_pos = dpo[...]
+    slot_pos = dot32(chooser, own_pos)
+    landed(r1_in)
+    bm_c.wait_recv()
+    bl_c.wait_recv()
+
+    mixed = jnp.concatenate([r1[s] for s in range(8)], axis=1)
+    encoded = kept + dot32(mixed, bm[...].reshape(1024, 1024))
+    lifted = dot32(norm_rows(encoded).astype(jnp.bfloat16), bl[...].reshape(1024, 512))
+    slot_in = (lifted + slot_pos).astype(jnp.bfloat16)
+    x_buf[z, y] = norm_rows(slot_in.astype(jnp.float32)).astype(jnp.bfloat16)
+    x_z = [send(x_buf.at[z, y], x_buf.at[z, y], (dp, peer)) for peer in z_peers]
+    x_y = [send(x_buf.at[z, y], x_buf.at[z, y], y_dev)]
+
+    def spread(row):
+        return jnp.transpose(chooser_of(row))
+
+    own_spread = spread(flag_row)
+    own_flag = jnp.sum(own_spread, axis=1, keepdims=True)
+    filled = dot32(own_spread.astype(jnp.bfloat16), slot_in)
+    dec_in = jnp.where(
+        own_flag > 0.5,
+        filled,
+        (mask_row + own_pos.astype(jnp.float32)).astype(jnp.bfloat16).astype(jnp.float32),
+    )
+    bd_y.wait_recv()
+    bd_x = send(bd.at[x, c], bd.at[x, c], x_dev)
+    for k in range(3):
+        x_z[k].wait_recv()
+        x_y.append(send(x_buf.at[z_from[k], y], x_buf.at[z_from[k], y], y_dev))
+    bp_x.wait_recv()
+    landed(x_y)
+    bp_y = send(bp.at[:, c, :, y], bp.at[:, c, :, y], y_dev)
+
+    slot_qkv = dot32(x_buf[...].reshape(512, 512), wd_all).astype(jnp.bfloat16)
+    for slab in range(8):
+        slab_spread = spread(flags_all[slab : slab + 1])
+        slab_flag = jnp.sum(slab_spread, axis=1, keepdims=True)
+        placed = dot32(slab_spread.astype(jnp.bfloat16), slot_qkv[slab * 64 : slab * 64 + 64])
+        qkv[slab * 128 : slab * 128 + 128, :] = jnp.where(
+            slab_flag > 0.5, placed, qm[slab].astype(jnp.float32)
+        ).astype(jnp.bfloat16)
+    bd_x.wait_recv()
+    bd_c = send(bd.at[:, c], bd.at[:, c], c_dev)
+
+    lane_q = lax.broadcasted_iota(jnp.int32, (256, 128), 1) // 32
+    lane_v = lax.broadcasted_iota(jnp.int32, (1024, 128), 1) // 32
+    key_rows = qkv[:, 128:256]
+    value_rows = qkv[:, 256:384]
+    scale = 1.0 / math.sqrt(32)
+
+    def dec_block(block, carry):
+        rows = pl.ds(pl.multiple_of(block * 256, 256), 256)
+        q_rows = qkv[rows, 0:128]
+        mix = jnp.zeros((256, 128), jnp.float32)
+        for head in range(2):
+            index = y * 2 + head
+            q_one = jnp.where(lane_q == index, q_rows, jnp.zeros_like(q_rows))
+            v_one = jnp.where(lane_v == index, value_rows, jnp.ones_like(value_rows))
+            scores = dot_nt(q_one, key_rows) * scale
+            top = jnp.max(scores, axis=-1, keepdims=True)
+            weights = jnp.exp(scores - top).astype(jnp.bfloat16)
+            summed = dot32(weights, v_one)
+            sums = jnp.where(y == 0, summed[:, 64:65], summed[:, 0:1])
+            mix = jnp.where(lane_q == index, summed / sums, mix)
+        m2[pl.ds(block * 2, 2)] = mix.astype(jnp.bfloat16).reshape(2, 128, 128)
+        return carry
+
+    lax.fori_loop(0, 4, dec_block, 0)
+    r2[sq] = m2[sq]
+    r2_in = [send(m2.at[peer], r2.at[sq], (dp, peer)) for peer in seq_peers]
+    bp_y.wait_recv()
+    bp_c = send(bp.at[:, c], bp.at[:, c], c_dev)
+    bd_c.wait_recv()
+    landed(r2_in)
+    dec_mixed = jnp.concatenate([r2[2 * j] + r2[2 * j + 1] for j in range(4)], axis=1)
+    decoded = (dec_in + dot32(dec_mixed, bd[...].reshape(512, 512))).astype(jnp.bfloat16)
+    dec_out[...] = decoded
+    final = norm_rows(decoded.astype(jnp.float32)).astype(jnp.bfloat16)
+    bp_c.wait_recv()
+    loss = jnp.zeros((128, 1), jnp.float32)
+    for piece in range(4):
+        cols = slice(piece * 1024, piece * 1024 + 1024)
+        predicted = dot32(final, bp[:, :, :, :, :, cols].reshape(512, 1024))
+        gap = predicted - (vx[:, cols].astype(jnp.float32) - vox_mean) * vox_scale
+        loss = loss + jnp.sum(gap * gap, axis=-1, keepdims=True)
+    loss_row = jnp.sum(
+        jnp.where(tok_col == tok_row, jnp.broadcast_to(loss * (1.0 / 4096), (128, 128)), 0.0),
+        axis=0,
+        keepdims=True,
+    )
+    loss_out[...] = jnp.where(flag_row > 0.5, 0.0, loss_row)
+    for copy in sent:
+        copy.wait_send()
+
+
+def fused_shards(
+    voxels,
+    patch_weight,
+    patch_bias,
+    enc_position,
+    visible,
+    enc_project,
+    enc_merge,
+    dec_lift,
+    mask_token,
+    dec_position,
+    dec_project,
+    dec_merge,
+    dec_predict,
+):
+    bf, f32 = jnp.bfloat16, jnp.float32
+    hbm = pl.BlockSpec(memory_space=pl.ANY)
+    vmem = pl.BlockSpec(memory_space=pltpu.VMEM)
+    decoded, loss = pl.pallas_call(
+        fused,
+        out_shape=(jax.ShapeDtypeStruct((128, 512), bf), jax.ShapeDtypeStruct((1, 128), f32)),
+        in_specs=[hbm, hbm, vmem, hbm, vmem, hbm, hbm, hbm, vmem, hbm, hbm, hbm, hbm],
+        out_specs=(vmem, vmem),
+        scratch_shapes=[
+            pltpu.VMEM((128, 4096), bf),
+            pltpu.VMEM((4096, 1024), bf),
+            pltpu.VMEM((128, 1024), bf),
+            pltpu.VMEM((128, 512), bf),
+            pltpu.VMEM((8, 8, 128), f32),
+            pltpu.VMEM((3, 2, 2, 8, 32, 128), bf),
+            pltpu.VMEM((3, 2, 2, 8, 16, 128), bf),
+            pltpu.VMEM((2, 2, 8, 32, 512), bf),
+            pltpu.VMEM((2, 2, 4, 2, 32, 1024), bf),
+            pltpu.VMEM((2, 2, 4, 2, 32, 512), bf),
+            pltpu.VMEM((2, 2, 4, 2, 16, 512), bf),
+            pltpu.VMEM((2, 2, 4, 2, 16, 4096), bf),
+            pltpu.VMEM((4, 2, 64, 1024), bf),
+            pltpu.VMEM((4, 2, 64, 512), bf),
+            pltpu.VMEM((8, 64, 128), bf),
+            pltpu.VMEM((8, 64, 128), bf),
+            pltpu.VMEM((8, 128, 128), bf),
+            pltpu.VMEM((8, 128, 128), bf),
+            pltpu.VMEM((8, 128, 384), bf),
+            pltpu.VMEM((1024, 384), bf),
+            pltpu.SemaphoreType.DMA((32,)),
+            pltpu.SemaphoreType.DMA((SENDS,)),
+            pltpu.SemaphoreType.DMA((SENDS,)),
+        ],
+        compiler_params=pltpu.CompilerParams(
+            collective_id=0, has_side_effects=True, vmem_limit_bytes=56 * 2**20
+        ),
+    )(
+        voxels.reshape(128, 4096),
+        patch_weight,
+        patch_bias.reshape(1, 1024),
+        enc_position,
+        visible,
+        enc_project,
+        enc_merge,
+        dec_lift,
+        mask_token.reshape(1, 512),
+        dec_position,
+        dec_project,
+        dec_merge,
+        dec_predict,
+    )
+    return decoded.reshape(1, 128, 512), loss
+
+
 def solution(mesh):
+    small = mesh.shape["dp"] == 4 and mesh.shape["seq"] == 8
     return jax.shard_map(
-        shards,
+        fused_shards if small else shards,
         mesh=mesh,
         in_specs=(
             P("dp", "seq", None),

time: 369 us -> 121 us (0.33)
  waiting for transfers between devices: 215 us -> 0 us
  Pallas kernels: 0 us -> 116 us
  blocking collectives: 73.7 us -> 0 us
  matrix products: 24.7 us -> 0 us
  starting transfers between devices: 22.8 us -> 0 us
  between operations: 14.2 us -> 0.64 us
  local copies, waits for them, and re-layouts: 10.9 us -> 2.74 us
  other arithmetic: 7.05 us -> 0 us
    all_gather x5 -> x0, waiting for transfers between devices: 184 us -> none  [the longest x1 56.8 us: shards(): lax.all_gather(enc_project, ('dp', 'seq'), axis=0, tiled=True)]
    pallas_call x0 -> x1, Pallas kernels: none -> 116 us  [fused_shards(): pl.pallas_call(fused, out_shape=(jax.ShapeDtypeStruct((128, 512), bf), ja...]
    all_gather x1 -> x0, blocking collectives: 73.7 us -> none  [shards(): lax.all_gather(dec_merge, ('dp', 'seq'), axis=0, tiled=True)]
    all_to_all x5 -> x0, waiting for transfers between devices: 27.6 us -> none  [the longest x2 14.9 us: shards(): lax.all_to_all(returning, 'seq', split_axis=0, concat_axis=0, tiled=True)]
    dot_general x19 -> x0, matrix products: 24.7 us -> none  [the longest x1 5.31 us: shards(): jnp.dot(chooser, embedded, preferred_element_type=jnp.float32)]
    all_to_all x5 -> x0, starting transfers between devices: 22.6 us -> none  [the longest x2 8.39 us: shards(): lax.all_to_all(outgoing, 'seq', split_axis=0, concat_axis=0, tiled=True)]
    reduce_sum x14 -> x0, other arithmetic: 5.42 us -> none  [the longest x6 2.52 us: one_block(): jnp.sum(exponent, axis=-1, keepdims=True)]
    reshape x9 -> x0, local copies, waits for them, and re-layouts: 4.02 us -> none  [the longest x3 1.71 us: place_rows(): return buffer.reshape(sources, all_rows // sources, flat_part.shape[1])]
  transfers between devices with their start and end apart: 10 -> 0, of which waited for: 7 -> 0; matrix products, arithmetic and copies ran while one was open for 11% -> 0% of each run, Pallas kernels for 0% -> 0%
where the time goes in v1:
time: 121 us; the launch traced here: 120 us
  Pallas kernels  116 us (96%)
  local copies, waits for them, and re-layouts  2.74 us (2%)
    pallas_call x1, Pallas kernels, fused_shards(): pl.pallas_call(fused, out_shape=(jax.ShapeDtypeStruct((128, 512), bf), ja...  116 us
    unnamed x2, local copies, waits for them, and re-layouts  2.74 us

profile of v1, /device:TPU:0, one launch (start us, length us, event | category | flops | bytes accessed | tf_op | source)
XLA Modules:
  0.0 119.5 jit_solution(4165356617593059389)
XLA Ops:
  0.6 116.1 %shard_map.140 = (bf16[128,512]{1,0:T(8,128)(2,1)}, f32[1,128]{1,0:T(1,128)}) custom-call(bf16[128,4096]{1,0:T(8,128)(2,1)} %bitcast.4, bf16[4096,1024]{1,0:T(8,128)(2,1)} %pw_hbm.1, f32[1,1024]{1,0:T(1,128)} %bitcast.6, bf16[128,1024]{1,0:T(8,128)(2,1)} %epos_hbm.1, s32[1,128]{1,0:T(1,128)} %vis_ref.1, bf16[32,3072]{1,0:T(8,128)(2,1)} %eproj_hbm.1, ...), custom_call_target="tpu_custom_call" | custom-call | tf_op jit(solution)/shard_map/pallas_call | solution.py:609
  116.8 1.6 %copy.17 = bf16[1,128,512]{2,1,0:T(8,128)(2,1)} copy(bf16[1,128,512]{2,1,0:T(8,128)(2,1)} %bitcast.5) | data formatting | bytes 262144
  118.3 1.2 copy.18

commit v2 on v1

--- a/solution.py
+++ b/solution.py
@@ -212,6 +212,7 @@
 
 
 PIECES = 4
+LOG2E = 1.4426950408889634
 SENDS = 160
 MESH = pl.DeviceIdType.MESH
 
@@ -243,7 +244,8 @@
     bm,
     bl,
     bd,
-    bp,
+    bpa,
+    bpb,
     e_buf,
     x_buf,
     m1,
@@ -320,8 +322,16 @@
                 wd.at[third, x, c, sq],
             )
         )
-    own.append(local(dpos_hbm.at[pl.ds(pl.multiple_of(dp * 32, 32), 32)], pos.at[x, c, sq]))
-    for part, buf in ((emerge_hbm, bm), (lift_hbm, bl), (dmerge_hbm, bd), (pred_hbm, bp)):
+    pos_part = dpos_hbm.at[pl.ds(pl.multiple_of(dp * 32, 32), 32)]
+    pred_a, pred_b = pred_hbm.at[:, pl.ds(0, 2048)], pred_hbm.at[:, pl.ds(2048, 2048)]
+    for part, buf in (
+        (emerge_hbm, bm),
+        (lift_hbm, bl),
+        (pos_part, pos),
+        (dmerge_hbm, bd),
+        (pred_a, bpa),
+        (pred_b, bpb),
+    ):
         own.append(local(part, buf.at[x, c, z, y]))
 
     flag_row = vis_ref[...].astype(jnp.float32)
@@ -334,7 +344,7 @@
     pl.semaphore_signal(barrier, inc=1, device_id=c_dev, device_id_type=MESH)
     pl.semaphore_wait(barrier, 9)
 
-    we_in, wd_in, pos_in, flags_in = [], [], [], []
+    we_in, wd_in, flags_in = [], [], []
     for peer in seq_peers:
         for third in range(3):
             we_in.append(
@@ -350,26 +360,20 @@
     def z_stage(part, buf):
         return [send(part, buf.at[x, c, z, y], (dp, peer)) for peer in z_peers]
 
+    def line(buf, device):
+        return send(buf.at[x, c, :, y], buf.at[x, c, :, y], device)
+
+    def sheet_x(buf):
+        return send(buf.at[x, c], buf.at[x, c], x_dev)
+
+    def sheet_y(buf):
+        return send(buf.at[:, c, :, y], buf.at[:, c, :, y], y_dev)
+
+    def half_c(buf):
+        return send(buf.at[:, c], buf.at[:, c], c_dev)
+
     bm_in = z_stage(emerge_hbm, bm)
     bl_in = z_stage(lift_hbm, bl)
-    for peer in seq_peers:
-        for third in range(3):
-            wd_in.append(
-                send(
-                    dproj_hbm.at[
-                        :, pl.ds(pl.multiple_of(third * 512 + (peer // 2) * 128, 128), 128)
-                    ],
-                    wd.at[third, x, c, sq],
-                    (dp, peer),
-                )
-            )
-    for peer in seq_peers:
-        pos_in.append(
-            send(
-                dpos_hbm.at[pl.ds(pl.multiple_of(dp * 32, 32), 32)], pos.at[x, c, sq], (dp, peer)
-            )
-        )
-
     tok_col = lax.broadcasted_iota(jnp.int32, (128, 128), 0)
     tok_row = lax.broadcasted_iota(jnp.int32, (128, 128), 1)
     upto = (tok_col <= tok_row).astype(jnp.bfloat16)
@@ -401,29 +405,42 @@
     e_z = [send(e_buf.at[z, y], e_buf.at[z, y], (dp, peer)) for peer in z_peers]
     e_y = [send(e_buf.at[z, y], e_buf.at[z, y], y_dev)]
 
+    for peer in seq_peers:
+        for third in range(3):
+            wd_in.append(
+                send(
+                    dproj_hbm.at[
+                        :, pl.ds(pl.multiple_of(third * 512 + (peer // 2) * 128, 128), 128)
+                    ],
+                    wd.at[third, x, c, sq],
+                    (dp, peer),
+                )
+            )
+    pos_in = z_stage(pos_part, pos)
+
     for copy in own:
         copy.wait()
     landed(we_in)
     we_x = send(we.at[:, x, c], we.at[:, x, c], x_dev)
+    landed(bl_in)
+    bl_x = line(bl, x_dev)
+    landed(bm_in)
+    bm_y = line(bm, y_dev)
 
     vox32 = vx[...].astype(jnp.float32)
     vox_mean = jnp.mean(vox32, axis=-1, keepdims=True)
     vox_centre = vox32 - vox_mean
     vox_scale = lax.rsqrt(jnp.mean(vox_centre * vox_centre, axis=-1, keepdims=True) + 1e-06)
 
+    we_x.wait_recv()
+    we_c = send(we.at[:, :, c], we.at[:, :, c], c_dev)
+    bm_y.wait_recv()
+    bm_x = sheet_x(bm)
     for k in range(3):
         e_z[k].wait_recv()
         e_y.append(send(e_buf.at[z_from[k], y], e_buf.at[z_from[k], y], y_dev))
-    we_x.wait_recv()
-    we_c = send(we.at[:, :, c], we.at[:, :, c], c_dev)
-    landed(bm_in)
-    bm_y = send(bm.at[x, c, :, y], bm.at[x, c, :, y], y_dev)
-    landed(bl_in)
-    bl_y = send(bl.at[x, c, :, y], bl.at[x, c, :, y], y_dev)
-    landed(wd_in)
-    wd_x = send(wd.at[:, x, c], wd.at[:, x, c], x_dev)
-    landed(pos_in)
-    pos_x = send(pos.at[x, c], pos.at[x, c], x_dev)
+    bl_x.wait_recv()
+    bl_y = sheet_y(bl)
     landed(flags_in)
     flags_all = jnp.max(flags_buf[...], axis=1)
     counts = jnp.sum(flags_all, axis=1, keepdims=True)
@@ -436,16 +453,9 @@
     )
     key_ok = (lane512[0:1] % 64).astype(jnp.float32) < count_row
     landed(e_y)
-    bm_y.wait_recv()
-    bm_x = send(bm.at[x, c], bm.at[x, c], x_dev)
-    bl_y.wait_recv()
-    bl_x = send(bl.at[x, c], bl.at[x, c], x_dev)
+    bpb_in = z_stage(pred_b, bpb)
+    bpa_in = z_stage(pred_a, bpa)
     bd_in = z_stage(dmerge_hbm, bd)
-    bp_in = z_stage(pred_hbm, bp)
-    wd_x.wait_recv()
-    wd_c = send(wd.at[:, :, c], wd.at[:, :, c], c_dev)
-    pos_x.wait_recv()
-    pos_c = send(pos.at[:, c], pos.at[:, c], c_dev)
     we_c.wait_recv()
 
     rows_in = e_buf[...].reshape(512, 1024)
@@ -458,10 +468,10 @@
         mine = lane128 // 64 == head
         q_one = jnp.where(mine, q_all, jnp.zeros_like(q_all))
         v_one = jnp.where(mine, v_all, jnp.ones_like(v_all))
-        scores = dot_nt(q_one, k_all) * (1.0 / 8.0)
-        scores = jnp.where(jnp.broadcast_to(key_ok, (512, 512)), scores, -1e30)
+        scores = dot_nt(q_one, k_all)
+        scores = jnp.where(jnp.broadcast_to(key_ok, (512, 512)), scores, -3e38)
         top = jnp.max(scores, axis=-1, keepdims=True)
-        weights = jnp.exp(scores - top).astype(jnp.bfloat16)
+        weights = jnp.exp2((scores - top) * (LOG2E / 8.0)).astype(jnp.bfloat16)
         summed = dot32(weights, v_one)
         spot = 64 * (1 - head)
         results.append(summed / summed[:, spot : spot + 1])
@@ -472,25 +482,24 @@
     r1_in = [send(m1.at[peer], r1.at[sq], (dp, peer)) for peer in seq_peers]
 
     bm_x.wait_recv()
-    bm_c = send(bm.at[:, c], bm.at[:, c], c_dev)
-    bl_x.wait_recv()
-    bl_c = send(bl.at[:, c], bl.at[:, c], c_dev)
-    wd_c.wait_recv()
-    pos_c.wait_recv()
-    wd_all = jnp.concatenate([wd[third].reshape(512, 128) for third in range(3)], axis=1)
+    bm_c = half_c(bm)
+    bl_y.wait_recv()
+    bl_c = half_c(bl)
+    landed(wd_in)
+    wd_x = send(wd.at[:, x, c], wd.at[:, x, c], x_dev)
+    landed(pos_in)
+    pos_y = line(pos, y_dev)
+    landed(bpb_in)
+    bpb_y = line(bpb, y_dev)
+    landed(bpa_in)
+    bpa_x = line(bpa, x_dev)
+    landed(bd_in)
+    bd_y = line(bd, y_dev)
+    wd_x.wait_recv()
+    wd_c = send(wd.at[:, :, c], wd.at[:, :, c], c_dev)
+    pos_y.wait_recv()
+    pos_x = sheet_x(pos)
     mask_row = mask_ref[...]
-
-    def masked_slab(slab, carry):
-        slab_pos = pos[:, :, slab].reshape(128, 512).astype(jnp.float32)
-        slab_in = (mask_row + slab_pos).astype(jnp.bfloat16).astype(jnp.float32)
-        qm[slab] = dot32(norm_rows(slab_in).astype(jnp.bfloat16), wd_all).astype(jnp.bfloat16)
-        return carry
-
-    lax.fori_loop(0, 8, masked_slab, 0)
-    landed(bp_in)
-    bp_x = send(bp.at[x, c, :, y], bp.at[x, c, :, y], x_dev)
-    landed(bd_in)
-    bd_y = send(bd.at[x, c, :, y], bd.at[x, c, :, y], y_dev)
     dpo_copy.wait()
     own_pos = dpo[...]
     slot_pos = dot32(chooser, own_pos)
@@ -509,6 +518,12 @@
     def spread(row):
         return jnp.transpose(chooser_of(row))
 
+    pos_x.wait_recv()
+    pos_c = half_c(pos)
+    bpb_y.wait_recv()
+    bpb_x = sheet_x(bpb)
+    bd_y.wait_recv()
+    bd_x = sheet_x(bd)
     own_spread = spread(flag_row)
     own_flag = jnp.sum(own_spread, axis=1, keepdims=True)
     filled = dot32(own_spread.astype(jnp.bfloat16), slot_in)
@@ -517,14 +532,23 @@
         filled,
         (mask_row + own_pos.astype(jnp.float32)).astype(jnp.bfloat16).astype(jnp.float32),
     )
-    bd_y.wait_recv()
-    bd_x = send(bd.at[x, c], bd.at[x, c], x_dev)
+    wd_c.wait_recv()
+    wd_all = jnp.concatenate([wd[third].reshape(512, 128) for third in range(3)], axis=1)
     for k in range(3):
         x_z[k].wait_recv()
         x_y.append(send(x_buf.at[z_from[k], y], x_buf.at[z_from[k], y], y_dev))
-    bp_x.wait_recv()
+    bpa_x.wait_recv()
+    bpa_y = sheet_y(bpa)
+    pos_c.wait_recv()
+
+    def masked_slab(slab, carry):
+        slab_pos = pos[:, :, slab // 2, slab % 2].reshape(128, 512).astype(jnp.float32)
+        slab_in = (mask_row + slab_pos).astype(jnp.bfloat16).astype(jnp.float32)
+        qm[slab] = dot32(norm_rows(slab_in).astype(jnp.bfloat16), wd_all).astype(jnp.bfloat16)
+        return carry
+
+    lax.fori_loop(0, 8, masked_slab, 0)
     landed(x_y)
-    bp_y = send(bp.at[:, c, :, y], bp.at[:, c, :, y], y_dev)
 
     slot_qkv = dot32(x_buf[...].reshape(512, 512), wd_all).astype(jnp.bfloat16)
     for slab in range(8):
@@ -535,13 +559,15 @@
             slab_flag > 0.5, placed, qm[slab].astype(jnp.float32)
         ).astype(jnp.bfloat16)
     bd_x.wait_recv()
-    bd_c = send(bd.at[:, c], bd.at[:, c], c_dev)
+    bd_c = half_c(bd)
+    bpb_x.wait_recv()
+    bpb_c = half_c(bpb)
 
     lane_q = lax.broadcasted_iota(jnp.int32, (256, 128), 1) // 32
     lane_v = lax.broadcasted_iota(jnp.int32, (1024, 128), 1) // 32
     key_rows = qkv[:, 128:256]
     value_rows = qkv[:, 256:384]
-    scale = 1.0 / math.sqrt(32)
+    scale = LOG2E / math.sqrt(32)
 
     def dec_block(block, carry):
         rows = pl.ds(pl.multiple_of(block * 256, 256), 256)
@@ -551,9 +577,9 @@
             index = y * 2 + head
             q_one = jnp.where(lane_q == index, q_rows, jnp.zeros_like(q_rows))
             v_one = jnp.where(lane_v == index, value_rows, jnp.ones_like(value_rows))
-            scores = dot_nt(q_one, key_rows) * scale
+            scores = dot_nt(q_one, key_rows)
             top = jnp.max(scores, axis=-1, keepdims=True)
-            weights = jnp.exp(scores - top).astype(jnp.bfloat16)
+            weights = jnp.exp2((scores - top) * scale).astype(jnp.bfloat16)
             summed = dot32(weights, v_one)
             sums = jnp.where(y == 0, summed[:, 64:65], summed[:, 0:1])
             mix = jnp.where(lane_q == index, summed / sums, mix)
@@ -563,21 +589,26 @@
     lax.fori_loop(0, 4, dec_block, 0)
     r2[sq] = m2[sq]
     r2_in = [send(m2.at[peer], r2.at[sq], (dp, peer)) for peer in seq_peers]
-    bp_y.wait_recv()
-    bp_c = send(bp.at[:, c], bp.at[:, c], c_dev)
+    bpa_y.wait_recv()
+    bpa_c = half_c(bpa)
     bd_c.wait_recv()
     landed(r2_in)
     dec_mixed = jnp.concatenate([r2[2 * j] + r2[2 * j + 1] for j in range(4)], axis=1)
     decoded = (dec_in + dot32(dec_mixed, bd[...].reshape(512, 512))).astype(jnp.bfloat16)
     dec_out[...] = decoded
     final = norm_rows(decoded.astype(jnp.float32)).astype(jnp.bfloat16)
-    bp_c.wait_recv()
     loss = jnp.zeros((128, 1), jnp.float32)
-    for piece in range(4):
-        cols = slice(piece * 1024, piece * 1024 + 1024)
-        predicted = dot32(final, bp[:, :, :, :, :, cols].reshape(512, 1024))
-        gap = predicted - (vx[:, cols].astype(jnp.float32) - vox_mean) * vox_scale
-        loss = loss + jnp.sum(gap * gap, axis=-1, keepdims=True)
+    for half, copy, start in ((bpb, bpb_c, 2048), (bpa, bpa_c, 0)):
+        copy.wait_recv()
+        for piece in range(2):
+            predicted = dot32(
+                final, half[:, :, :, :, :, piece * 1024 : piece * 1024 + 1024].reshape(512, 1024)
+            )
+            base = start + piece * 1024
+            gap = (
+                predicted - (vx[:, base : base + 1024].astype(jnp.float32) - vox_mean) * vox_scale
+            )
+            loss = loss + jnp.sum(gap * gap, axis=-1, keepdims=True)
     loss_row = jnp.sum(
         jnp.where(tok_col == tok_row, jnp.broadcast_to(loss * (1.0 / 4096), (128, 128)), 0.0),
         axis=0,
@@ -619,11 +650,12 @@
             pltpu.VMEM((8, 8, 128), f32),
             pltpu.VMEM((3, 2, 2, 8, 32, 128), bf),
             pltpu.VMEM((3, 2, 2, 8, 16, 128), bf),
-            pltpu.VMEM((2, 2, 8, 32, 512), bf),
+            pltpu.VMEM((2, 2, 4, 2, 32, 512), bf),
             pltpu.VMEM((2, 2, 4, 2, 32, 1024), bf),
             pltpu.VMEM((2, 2, 4, 2, 32, 512), bf),
             pltpu.VMEM((2, 2, 4, 2, 16, 512), bf),
-            pltpu.VMEM((2, 2, 4, 2, 16, 4096), bf),
+            pltpu.VMEM((2, 2, 4, 2, 16, 2048), bf),
+            pltpu.VMEM((2, 2, 4, 2, 16, 2048), bf),
             pltpu.VMEM((4, 2, 64, 1024), bf),
             pltpu.VMEM((4, 2, 64, 512), bf),
             pltpu.VMEM((8, 64, 128), bf),

time: 121 us -> 105 us (0.87); the launches traced: 120 us -> 105 us
  Pallas kernels: 116 us -> 102 us
    pallas_call x1, Pallas kernels: 116 us -> 102 us  [fused_shards(): pl.pallas_call(fused, out_shape=(jax.ShapeDtypeStruct((128, 512), bf), ja...]
where the time goes in v2:
time: 105 us
  Pallas kernels  102 us (97%)
  local copies, waits for them, and re-layouts  2.74 us (3%)
    pallas_call x1, Pallas kernels, fused_shards(): pl.pallas_call(fused, out_shape=(jax.ShapeDtypeStruct((128, 512), bf), ja...  102 us
    unnamed x2, local copies, waits for them, and re-layouts  2.74 us

profile of v2, /device:TPU:0, one launch (start us, length us, event | category | flops | bytes accessed | tf_op | source)
XLA Modules:
  0.0 104.9 jit_solution(16848474940758032607)
XLA Ops:
  0.6 101.5 %shard_map.140 = (bf16[128,512]{1,0:T(8,128)(2,1)}, f32[1,128]{1,0:T(1,128)}) custom-call(bf16[128,4096]{1,0:T(8,128)(2,1)} %bitcast.4, bf16[4096,1024]{1,0:T(8,128)(2,1)} %pw_hbm.1, f32[1,1024]{1,0:T(1,128)} %bitcast.6, bf16[128,1024]{1,0:T(8,128)(2,1)} %epos_hbm.1, s32[1,128]{1,0:T(1,128)} %vis_ref.1, bf16[32,3072]{1,0:T(8,128)(2,1)} %eproj_hbm.1, ...), custom_call_target="tpu_custom_call" | custom-call | tf_op jit(solution)/shard_map/pallas_call | solution.py:640
  102.1 1.6 %copy.17 = bf16[1,128,512]{2,1,0:T(8,128)(2,1)} copy(bf16[1,128,512]{2,1,0:T(8,128)(2,1)} %bitcast.5) | data formatting | bytes 262144
  103.7 1.2 %copy.18 = f32[1,128]{1,0:T(1,128)} copy(f32[1,128]{1,0:T(1,128)} %get-tuple-element.9) | data formatting | bytes 1024
